TPU v7x, 128 devices: a whole 4x4x4 slice. The times are simulated.
128 devices in a mesh: dp: 16 (over z, y), tensor: 8 (over x, core).
Axes of the slice: x: 4, y: 4, z: 4, core: 2. Of those that a mesh axis runs over, the one named last changes fastest.
Arguments:
- tile_tokens: bfloat16 [256, 256, 1536], P('dp'), may hold values from -6 to 6
- vit_qkv: bfloat16 [1536, 24, 3, 64], P(None, 'tensor'), as said below
- vit_out: bfloat16 [1536, 1536], P('tensor'), may hold values from -0.15625 to 0.15625
- tile_norm_gain: bfloat16 [1536], replicated, may hold values from 0.099609375 to 1.8984375
- fresh_proj: bfloat16 [1536, 768], replicated, may hold values from -0.15625 to 0.15625
- tile_target: int32 [256], replicated, may hold values from 0 to 16383
- cached_rows: bfloat16 [16384, 768], P(('dp', 'tensor')), may hold values from -6 to 6
- slide_tiles: int32 [4], replicated, may hold values from 1 to 8192, 16384 in all
- head_shift: int32 [16], replicated, may hold values from 0 to 15
- long_gain: bfloat16 [768], replicated, may hold values from 0.099609375 to 1.8984375
- long_qkv: bfloat16 [768, 16, 3, 48], replicated, as said below
- long_out: bfloat16 [768, 768], replicated, may hold values from -0.21875 to 0.21875
Outputs:
- slide_output: bfloat16 [16384, 768], P(('dp', 'tensor'))
Inputs may be any that keep to these rules, and one draw needn't show every extreme that they name: `slide_tiles`: the counts sum to 16384; the largest is exactly 8192. `tile_target`: rows may repeat. `vit_qkv`: dense projection entries. `long_qkv`: dense projection entries.
All inputs are finite; a program needn't handle non-finite values.
Results may differ from a plain program's by a relative error of at most 0.006.
Values may be sent and summed in bfloat16 or wider, within the bound.
A program may use at most 192 MiB of HBM per device.

v0:
```python
import functools
import math

import jax
import jax.numpy as jnp
from jax import lax
from jax.experimental import pallas as pl
from jax.experimental.pallas import tpu as pltpu
from jax.sharding import PartitionSpec as P

MESH = pl.DeviceIdType.MESH
EPSILON = 1e-06
OUTSIDE = -1e30
LOG2E = 1.4426950408889634
NN = (((1,), (0,)), ((), ()))
NT = (((1,), (1,)), ((), ()))
TN = (((0,), (0,)), ((), ()))
F32 = jnp.float32
BF16 = jnp.bfloat16

TILES_HERE = 16
TOK = 256
D = 1536
VH_HERE = 3
VS = 64
VW = VH_HERE * 3 * VS
LD = 768
LH = 16
LS = 48
LW = 3 * LS
ROWS = 128
SEG = 1024
CHUNK = 2048
KX = 64
VIT_SCALE = LOG2E / math.sqrt(VS)
LONG_SCALE = LOG2E / math.sqrt(LS)


def dot(a, b, dims=NN):
    return lax.dot_general(a, b, dims, preferred_element_type=F32)


def iota(shape, dim):
    return lax.broadcasted_iota(jnp.int32, shape, dim)


def split3(value):
    high = value.astype(BF16)
    rest = value - high.astype(F32)
    middle = rest.astype(BF16)
    low = (rest - middle.astype(F32)).astype(BF16)
    return high, middle, low


def tile_kernel(x_ref, w_ref, pooled_ref, mean_ref, wext, csum):
    step = pl.program_id(0)
    tensor = lax.axis_index("tensor")

    @pl.when(step == 0)
    def _():
        wext[0:VW, :] = w_ref[...]
        row = iota((16, D), 0)
        col = iota((16, D), 1)
        extra = jnp.where(row == 0, 1.0, jnp.where((row == 1) & (col == 0), 1.0, 0.0))
        wext[VW : VW + 16, :] = extra.astype(BF16)
        csum[...] = dot(w_ref[...], jnp.ones((D, TOK), BF16))

    x = x_ref[0]
    raw = dot(wext[...], x, NT)
    mean = raw[VW : VW + 1] * (1.0 / D)
    first_row = raw[VW + 1 : VW + 2]
    first = x[:, 0:1].astype(F32)
    squares = jnp.zeros((TOK, 128), F32)
    for k in range(D // 128):
        delta = x[:, 128 * k : 128 * (k + 1)].astype(F32) - first
        squares = squares + delta * delta
    high, middle, low = split3(squares)
    ones = jnp.ones((16, 128), BF16)
    total = dot(ones, high, NT) + dot(ones, middle, NT) + dot(ones, low, NT)
    shift = mean - first_row
    variance = jnp.maximum(total[0:1] * (1.0 / D) - shift * shift, 0.0)
    scale = lax.rsqrt(variance + EPSILON)
    projected = ((raw[0:VW] - csum[...] * mean) * scale).astype(BF16)
    attended = []
    for head in range(VH_HERE):
        base = head * 3 * VS
        query = projected[base : base + VS]
        key = projected[base + VS : base + 2 * VS]
        value = projected[base + 2 * VS : base + 3 * VS]
        scores = dot(key, query, TN)
        highest = jnp.max(scores, axis=0, keepdims=True)
        weights = jnp.exp2((scores - highest) * VIT_SCALE)
        sums = jnp.sum(weights, axis=0, keepdims=True)
        mixture = dot(value, weights.astype(BF16))
        attended.append((mixture / sums).astype(BF16))
    attended = jnp.concatenate(attended, axis=0)
    pooled = dot(jnp.ones((16, TOK), BF16), attended, NT) * (1.0 / TOK)
    pooled_ref[pl.ds(step, 1), :] = pooled[0:1]

    @pl.when(step // 2 == tensor)
    def _():
        sums = dot(jnp.ones((16, TOK), BF16), x) * (1.0 / TOK)
        mean_ref[pl.ds(step % 2, 1), :] = sums[0:1]


def encode_tiles(tokens, weights):
    return pl.pallas_call(
        tile_kernel,
        grid=(TILES_HERE,),
        in_specs=[
            pl.BlockSpec((1, TOK, D), lambda i: (i, 0, 0)),
            pl.BlockSpec((VW, D), lambda i: (0, 0)),
        ],
        out_specs=[
            pl.BlockSpec((TILES_HERE, VH_HERE * VS), lambda i: (0, 0)),
            pl.BlockSpec((8, D), lambda i: (0, 0)),
        ],
        out_shape=[
            jax.ShapeDtypeStruct((TILES_HERE, VH_HERE * VS), F32),
            jax.ShapeDtypeStruct((8, D), F32),
        ],
        scratch_shapes=[pltpu.VMEM((VW + 16, D), BF16), pltpu.VMEM((VW, TOK), F32)],
        compiler_params=pltpu.CompilerParams(vmem_limit_bytes=32 * 1024 * 1024),
    )(tokens, weights)


def normalize_rows(values):
    center = values - jnp.mean(values, axis=-1, keepdims=True)
    return center * lax.rsqrt(jnp.mean(center * center, axis=-1, keepdims=True) + EPSILON)


def bit_reversed(rank):
    return (rank % 2) * 8 + (rank // 2 % 2) * 4 + (rank // 4 % 2) * 2 + rank // 8


def slide_kernel(
    pooled_ref,
    tile_mean_ref,
    vit_out_hbm,
    tile_gain_ref,
    fresh_proj_hbm,
    target_ref,
    cached_hbm,
    slide_tiles_ref,
    head_shift_ref,
    long_gain_ref,
    long_qkv_hbm,
    long_out_hbm,
    out_ref,
    vit_out,
    fresh_proj,
    cached,
    long_qkv,
    long_out,
    part,
    part_in,
    fresh_in,
    fresh_all,
    seq,
    hidden,
    packed,
    qkv,
    perm,
    qx,
    kx,
    vx,
    send2,
    send3,
    send4,
    got2,
    got3,
    got4,
    num,
    top,
    mix_out,
    mix_in,
    load_sem,
    sems,
):
    d = lax.axis_index("dp")
    t = lax.axis_index("tensor")
    chunk = d // 2
    half = d % 2
    mine = half * 8 + t

    used = [0]

    def remote(src, dst, device):
        i = used[0]
        used[0] += 1
        return pltpu.make_async_remote_copy(
            src_ref=src,
            dst_ref=dst,
            send_sem=sems.at[0, i],
            recv_sem=sems.at[1, i],
            device_id=device,
            device_id_type=MESH,
        )

    barrier = pltpu.get_barrier_semaphore()
    for k in range(1, 8):
        pl.semaphore_signal(barrier, 1, device_id=(d, (t + k) % 8), device_id_type=MESH)
        pl.semaphore_signal(
            barrier, 1, device_id=(2 * chunk + 1 - half, (t + k) % 8), device_id_type=MESH
        )
    for k in range(1, 16):
        pl.semaphore_signal(barrier, 1, device_id=((d + k) % 16, t), device_id_type=MESH)

    loads = [
        pltpu.make_async_copy(src, dst, load_sem.at[i])
        for i, (src, dst) in enumerate(
            [
                (vit_out_hbm, vit_out),
                (fresh_proj_hbm, fresh_proj),
                (cached_hbm, cached),
                (long_qkv_hbm, long_qkv),
                (long_out_hbm, long_out),
            ]
        )
    ]
    for load in loads:
        load.start()

    loads[0].wait()
    high, middle, low = split3(pooled_ref[...])
    weight = vit_out[...]
    partial = dot(high, weight) + dot(middle, weight) + dot(low, weight)
    for k in range(8):
        part[k] = partial[2 * k : 2 * k + 2]
    pl.semaphore_wait(barrier, 29)
    reduce_copies = []
    for k in range(1, 8):
        peer = (t + k) % 8
        copy = remote(part.at[peer], part_in.at[t], (d, peer))
        copy.start()
        reduce_copies.append(copy)
    part_in[pl.ds(t, 1)] = part[pl.ds(t, 1)]

    shift = head_shift_ref[mine] % 16
    place = iota((SEG, 1), 0)
    goal = bit_reversed((place + 16 - shift) % 16) * 64 + place // 16
    perm[...] = jnp.where(goal == iota((SEG, SEG), 1), 1.0, 0.0).astype(BF16)
    end0 = slide_tiles_ref[0]
    end1 = end0 + slide_tiles_ref[1]
    end2 = end1 + slide_tiles_ref[2]

    def slides(count, width, which):
        lane = iota((16, count), 1)
        spot = lane % width
        row = (
            SEG * (2 * which + lane // width)
            + 16 * (spot % 64)
            + (bit_reversed(spot // 64) + shift) % 16
        )
        return (
            (row >= end0).astype(jnp.int32)
            + (row >= end1).astype(jnp.int32)
            + (row >= end2).astype(jnp.int32)
        )

    def query_marks(count, width, which):
        ids = slides(count, width, which)
        return jnp.where(ids == iota(ids.shape, 0), 1.0, 0.0).astype(BF16)

    def key_marks(count, width, which):
        ids = slides(count, width, which)
        feature = iota(ids.shape, 0)
        return jnp.where((feature < 4) & (ids != feature), OUTSIDE, 0.0).astype(BF16)

    def value_marks(count):
        return jnp.where(iota((16, count), 0) == 0, 1.0, 0.0).astype(BF16)

    for copy in reduce_copies:
        copy.wait_recv()
    pooled = tile_mean_ref[0:2, :]
    for k in range(8):
        pooled = pooled + part_in[k]
    normed = (normalize_rows(pooled) * tile_gain_ref[...].astype(F32)).astype(BF16)
    loads[1].wait()
    fresh = dot(normed, fresh_proj[...])
    fresh_in[pl.ds(t, 1)] = fresh[None]
    gather_copies = []
    for k in range(1, 8):
        copy = remote(fresh_in.at[t], fresh_in.at[t], (d, (t + k) % 8))
        copy.start()
        gather_copies.append(copy)
    for copy in gather_copies:
        copy.wait_recv()
    group = jnp.concatenate([fresh_in[k] for k in range(8)], axis=0).astype(BF16)
    here = pl.ds(pl.multiple_of(d * 16, 16), 16)
    fresh_all[here, :] = group
    spread_copies = []
    for k in range(1, 16):
        copy = remote(fresh_all.at[here], fresh_all.at[here], ((d + k) % 16, t))
        copy.start()
        spread_copies.append(copy)
    first_row = (d * 8 + t) * ROWS
    match = (target_ref[...] - first_row == iota((ROWS, 256), 0))
    match = jnp.where(match, 1.0, 0.0).astype(BF16)
    loads[2].wait()
    for copy in spread_copies:
        copy.wait_recv()
    rows = cached[...].astype(F32) + dot(match, fresh_all[...])
    seq[...] = rows
    hidden[...] = (normalize_rows(rows) * long_gain_ref[...].astype(F32)).astype(BF16)

    loads[3].wait()
    head_copies = []
    for k in range(1, 17):
        head = (mine + k) % 16
        weight = long_qkv[pl.ds(pl.multiple_of(head * LW, LW), LW), :]
        block = dot(weight, hidden[...], NT).astype(BF16)
        lanes = pl.ds(pl.multiple_of(mine * ROWS, ROWS), ROWS)
        if k == 16:
            qkv[:, lanes] = block
        else:
            packed[k - 1] = block
            copy = remote(
                packed.at[k - 1], qkv.at[:, lanes], (2 * chunk + head // 8, head % 8)
            )
            copy.start()
            head_copies.append(copy)
    for copy in head_copies:
        copy.wait_recv()

    low_half = iota((LW, 128), 1) < 64
    sides = []
    for side in range(2):
        lanes = slice(side * SEG, (side + 1) * SEG)
        ordered = dot(qkv[:, lanes], perm[...])
        sides.append(ordered[:, 0:128])
        ordered = ordered.astype(BF16)
        qx[0:LS, lanes] = ordered[0:LS]
        kx[0:LS, lanes] = ordered[LS : 2 * LS]
        vx[0:LS, lanes] = ordered[2 * LS : LW]
        send2[:, side * 256 : (side + 1) * 256] = ordered[LS:LW, 0:256]
        send3[:, side * 128 : (side + 1) * 128] = ordered[LS:LW, 0:128]
    both = jnp.where(low_half, sides[0], pltpu.roll(sides[1], 64, 1)).astype(BF16)
    send4[...] = both[LS:LW]
    quad = chunk // 4
    inner = chunk % 4
    far_copies = [
        remote(send2, got2, (2 * (chunk + 1 - 2 * (chunk % 2)) + half, t))
    ]
    for k in range(2):
        other = quad * 4 + (1 - inner // 2) * 2 + (inner % 2 + k) % 2
        far_copies.append(remote(send3, got3.at[k], (2 * other + half, t)))
    for k in range(4):
        other = (1 - quad) * 4 + (inner + k) % 4
        far_copies.append(remote(send4, got4.at[k], (2 * other + half, t)))
    for copy in far_copies:
        copy.start()

    qx[LS:KX, :] = query_marks(CHUNK, SEG, chunk)
    kx[LS:KX, :] = key_marks(CHUNK, SEG, chunk)
    vx[LS:KX, :] = value_marks(CHUNK)

    def attend(keys, values, queries):
        scores = dot(keys, queries, TN)
        highest = jnp.max(scores, axis=0, keepdims=True)
        weights = jnp.exp2((scores - highest) * LONG_SCALE).astype(BF16)
        return dot(values, weights), highest

    def merge(lanes, other_num, other_top):
        old_top = top[0:1, lanes]
        new_top = jnp.maximum(old_top, other_top)
        num[:, lanes] = num[:, lanes] * jnp.exp2(
            (old_top - new_top) * LONG_SCALE
        ) + other_num * jnp.exp2((other_top - new_top) * LONG_SCALE)
        top[0:1, lanes] = new_top

    def first_pair(i, carry):
        for side in range(2):
            lanes = slice(side * SEG, (side + 1) * SEG)
            spot = pl.ds(pl.multiple_of(side * SEG + i * 256, 256), 256)
            result, highest = attend(kx[:, lanes], vx[:, lanes], qx[:, spot])
            num[:, spot] = result
            top[0:1, spot] = highest
        return carry

    lax.fori_loop(0, 4, first_pair, 0)

    def joined(ref, width):
        return jnp.concatenate([ref[:, 0:width], ref[:, SEG : SEG + width]], axis=1)

    keys = joined(kx, 512)
    values = joined(vx, 512)
    for side in range(2):
        for i in range(2):
            lanes = slice(side * SEG + i * 256, side * SEG + (i + 1) * 256)
            merge(lanes, *attend(keys, values, qx[:, lanes]))

    def arrived(block, count, width, which):
        key = jnp.concatenate([block[0:LS], key_marks(count, width, which)], axis=0)
        value = jnp.concatenate([block[LS : 2 * LS], value_marks(count)], axis=0)
        return key, value

    for copy in far_copies:
        copy.wait_recv()
    beside = chunk + 1 - 2 * (chunk % 2)
    key2, value2 = arrived(got2[...], 512, 256, beside)
    keys = jnp.concatenate([joined(kx, 256), key2], axis=1)
    values = jnp.concatenate([joined(vx, 256), value2], axis=1)
    for side in range(2):
        lanes = slice(side * SEG, side * SEG + 256)
        merge(lanes, *attend(keys, values, qx[:, lanes]))

    keys3 = [joined(kx, 128), key2[:, 0:128], key2[:, 256:384]]
    values3 = [joined(vx, 128), value2[:, 0:128], value2[:, 256:384]]
    for k in range(2):
        other = quad * 4 + (1 - inner // 2) * 2 + (inner % 2 + k) % 2
        key, value = arrived(got3[k], 256, 128, other)
        keys3.append(key)
        values3.append(value)
    keys = jnp.concatenate(keys3, axis=1)
    values = jnp.concatenate(values3, axis=1)
    result, highest = attend(keys, values, joined(qx, 128))
    merge(slice(0, 128), result[:, 0:128], highest[:, 0:128])
    merge(slice(SEG, SEG + 128), result[:, 128:256], highest[:, 128:256])

    lower = iota((KX, 128), 1) < 64

    def packed_pair(a, b):
        moved = pltpu.roll(b.astype(F32), 64, 1)
        return jnp.where(lower, a.astype(F32), moved).astype(BF16)

    keys4 = []
    values4 = []
    for blocks, gather in ((keys3, keys4), (values3, values4)):
        own = blocks[0]
        gather.append(packed_pair(own[:, 0:128], own[:, 128:256]))
        gather.append(packed_pair(blocks[1], blocks[2]))
        for k in range(2):
            far = blocks[3 + k]
            gather.append(packed_pair(far[:, 0:128], far[:, 128:256]))
    for k in range(4):
        other = (1 - quad) * 4 + (inner + 4 - k) % 4
        key, value = arrived(got4[k], 128, 64, other)
        keys4.append(key)
        values4.append(value)
    keys = jnp.concatenate(keys4, axis=1)
    values = jnp.concatenate(values4, axis=1)
    query = packed_pair(qx[:, 0:128], qx[:, SEG : SEG + 128])
    result, highest = attend(keys, values, query)
    highest = jnp.broadcast_to(highest, (8, 128))
    for side in range(2):
        if side == 1:
            result = pltpu.roll(result, 64, 1)
            highest = pltpu.roll(highest, 64, 1)
        lanes = slice(side * SEG, side * SEG + 128)
        merge(
            lanes,
            jnp.where(lower, result, 0.0),
            jnp.where(lower[0:1], highest[0:1], OUTSIDE),
        )

    mix_copies = []
    for side in range(2):
        lanes = slice(side * SEG, (side + 1) * SEG)
        blended = (num[0:LS, lanes] / num[LS : LS + 1, lanes]).astype(BF16)
        natural = dot(blended, perm[...], NT).astype(BF16)
        for i in range(8):
            mix_out[side * 8 + i] = natural[:, i * ROWS : (i + 1) * ROWS]
    for k in range(1, 16):
        device = (mine + k) % 16
        copy = remote(
            mix_out.at[device],
            mix_in.at[mine],
            (2 * chunk + device // 8, device % 8),
        )
        copy.start()
        mix_copies.append(copy)
    mix_in[pl.ds(mine, 1)] = mix_out[pl.ds(mine, 1)]
    loads[4].wait()
    for copy in mix_copies:
        copy.wait_recv()
    mixture = mix_in[...].reshape(LD, ROWS)
    out_ref[...] = (seq[...] + dot(mixture, long_out[...], TN)).astype(BF16)

    for copies in (
        reduce_copies, gather_copies, spread_copies, head_copies, far_copies, mix_copies
    ):
        for copy in copies:
            copy.wait_send()


def slide_layer(*arguments):
    vmem = pl.BlockSpec(memory_space=pltpu.VMEM)
    smem = pl.BlockSpec(memory_space=pltpu.SMEM)
    hbm = pl.BlockSpec(memory_space=pl.ANY)
    return pl.pallas_call(
        slide_kernel,
        out_shape=jax.ShapeDtypeStruct((ROWS, LD), BF16),
        in_specs=[vmem, vmem, hbm, vmem, hbm, vmem, hbm, smem, smem, vmem, hbm, hbm],
        out_specs=vmem,
        scratch_shapes=[
            pltpu.VMEM((VH_HERE * VS, D), BF16),
            pltpu.VMEM((D, LD), BF16),
            pltpu.VMEM((ROWS, LD), BF16),
            pltpu.VMEM((LH * LW, LD), BF16),
            pltpu.VMEM((LD, LD), BF16),
            pltpu.VMEM((8, 2, D), F32),
            pltpu.VMEM((8, 2, D), F32),
            pltpu.VMEM((8, 2, LD), F32),
            pltpu.VMEM((256, LD), BF16),
            pltpu.VMEM((ROWS, LD), F32),
            pltpu.VMEM((ROWS, LD), BF16),
            pltpu.VMEM((15, LW, ROWS), BF16),
            pltpu.VMEM((LW, CHUNK), BF16),
            pltpu.VMEM((SEG, SEG), BF16),
            pltpu.VMEM((KX, CHUNK), BF16),
            pltpu.VMEM((KX, CHUNK), BF16),
            pltpu.VMEM((KX, CHUNK), BF16),
            pltpu.VMEM((2 * LS, 512), BF16),
            pltpu.VMEM((2 * LS, 256), BF16),
            pltpu.VMEM((2 * LS, 128), BF16),
            pltpu.VMEM((2 * LS, 512), BF16),
            pltpu.VMEM((2, 2 * LS, 256), BF16),
            pltpu.VMEM((4, 2 * LS, 128), BF16),
            pltpu.VMEM((KX, CHUNK), F32),
            pltpu.VMEM((8, CHUNK), F32),
            pltpu.VMEM((16, LS, ROWS), BF16),
            pltpu.VMEM((16, LS, ROWS), BF16),
            pltpu.SemaphoreType.DMA((5,)),
            pltpu.SemaphoreType.DMA((2, 66)),
        ],
        compiler_params=pltpu.CompilerParams(
            collective_id=0,
            has_side_effects=True,
            vmem_limit_bytes=48 * 1024 * 1024,
        ),
    )(*arguments)


def body(
    tile_tokens,
    vit_qkv,
    vit_out,
    tile_norm_gain,
    fresh_proj,
    tile_target,
    cached_rows,
    slide_tiles,
    head_shift,
    long_gain,
    long_qkv,
    long_out,
):
    vit_rows = jnp.transpose(vit_qkv, (1, 2, 3, 0)).reshape(VW, D)
    long_rows = jnp.transpose(long_qkv, (1, 2, 3, 0)).reshape(LH * LW, LD)
    pooled, tile_means = encode_tiles(tile_tokens, vit_rows)
    return slide_layer(
        pooled,
        tile_means,
        vit_out,
        tile_norm_gain.reshape(1, D),
        fresh_proj,
        tile_target.reshape(1, 256),
        cached_rows,
        slide_tiles,
        head_shift,
        long_gain.reshape(1, LD),
        long_rows,
        long_out,
    )


def solution(mesh):
    placed = (
        P("dp", None, None),
        P(None, "tensor", None, None),
        P("tensor", None),
        P(),
        P(),
        P(),
        P(("dp", "tensor"), None),
        P(),
        P(),
        P(),
        P(),
        P(),
    )
    return jax.shard_map(
        body, mesh=mesh, in_specs=placed, out_specs=P(("dp", "tensor"), None), check_vma=False
    )
```

profile of v0, /device:TPU:1, one launch (start us, length us, event | category | flops | bytes accessed | tf_op | source)
XLA Modules:
  0.0 96.7 jit_solution(17108876243216691763)
XLA Ops:
  0.0 0.7 reshape.18.long_gain_ref
  0.7 0.7 reshape.16.tile_gain_ref
  1.4 0.0 copy-start
  1.4 4.6 %copy-done = bf16[16,256,1536]{2,1,0:T(8,128)(2,1)S(1)} copy-done((bf16[16,256,1536]{2,1,0:T(8,128)(2,1)S(1)}, bf16[16,256,1536]{2,1,0:T(8,128)(2,1)}, u32[]{:S(2)}) %copy-start) | copy-done | bytes 12582936
  6.0 0.0 copy-start.2
  6.0 1.5 %copy-done.2 = bf16[1536,3,3,64]{0,3,2,1:T(8,128)(2,1)S(1)} copy-done((bf16[1536,3,3,64]{0,3,2,1:T(8,128)(2,1)S(1)}, bf16[1536,3,3,64]{0,3,2,1:T(8,128)(2,1)}, u32[]{:S(2)}) %copy-start.2) | copy-done | bytes 1769496
  7.4 0.0 copy-start.1
  7.4 0.0 copy-start.3
  7.4 0.0 copy-start.4
  7.4 0.0 copy-start.5
  7.4 0.0 copy-start.6
  7.5 0.0 copy-start.7
  7.5 0.0 copy-start.8
  7.5 34.3 %shard_map.118 = (f32[16,192]{1,0:T(8,128)S(1)}, f32[8,1536]{1,0:T(8,128)S(1)}) custom-call(bf16[16,256,1536]{2,1,0:T(8,128)(2,1)S(1)} %copy-done, bf16[576,1536]{1,0:T(8,128)(2,1)S(1)} %bitcast.7), custom_call_target="tpu_custom_call" | custom-call | tf_op jit(solution)/shard_map/pallas_call | solution.py:107
  41.7 0.0 copy-done.1
  41.7 0.0 copy-done.3
  41.7 0.0 copy-done.4
  41.7 0.0 copy-done.5
  41.8 0.0 copy-done.6
  41.8 0.0 copy-done.7
  41.8 0.0 copy-done.8
  41.8 54.2 %shard_map.119 = bf16[128,768]{1,0:T(8,128)(2,1)S(1)} custom-call(f32[16,192]{1,0:T(8,128)S(1)} %get-tuple-element.7.pooled_ref, f32[8,1536]{1,0:T(8,128)S(1)} %get-tuple-element.8.tile_mean_ref, bf16[192,1536]{1,0:T(8,128)(2,1)S(1)} %copy-done.4, bf16[1,1536]{1,0:T(2,128)(2,1)S(1)} %reshape.16.tile_gain_ref, bf16[1536,768]{1,0:T(8,128)(2,1)S(1)} %copy-done.1, ...), custom_call_target="tpu_custom_call" | custom-call | tf_op jit(solution)/shard_map/pallas_call | solution.py:491
  96.0 0.7 copy.14
Async XLA Ops:
  1.4 4.6 %copy-start = (bf16[16,256,1536]{2,1,0:T(8,128)(2,1)S(1)}, bf16[16,256,1536]{2,1,0:T(8,128)(2,1)}, u32[]{:S(2)}) copy-start(bf16[16,256,1536]{2,1,0:T(8,128)(2,1)} %x_ref.1) | copy-start | bytes 37748740
  6.0 1.5 %copy-start.2 = (bf16[1536,3,3,64]{0,3,2,1:T(8,128)(2,1)S(1)}, bf16[1536,3,3,64]{0,3,2,1:T(8,128)(2,1)}, u32[]{:S(2)}) copy-start(bf16[1536,3,3,64]{0,3,2,1:T(8,128)(2,1)} %param.13) | copy-start | bytes 5308420
  7.4 34.3 %copy-start.1 = (bf16[1536,768]{1,0:T(8,128)(2,1)S(1)}, bf16[1536,768]{1,0:T(8,128)(2,1)}, u32[]{:S(2)}) copy-start(bf16[1536,768]{1,0:T(8,128)(2,1)} %fresh_proj_hbm.1) | copy-start | bytes 7077892
  7.4 34.3 %copy-start.3 = (bf16[768,768]{1,0:T(8,128)(2,1)S(1)}, bf16[768,768]{1,0:T(8,128)(2,1)}, u32[]{:S(2)}) copy-start(bf16[768,768]{1,0:T(8,128)(2,1)} %long_out_hbm.1) | copy-start | bytes 3538948
  7.4 34.3 %copy-start.4 = (bf16[192,1536]{1,0:T(8,128)(2,1)S(1)}, bf16[192,1536]{1,0:T(8,128)(2,1)}, u32[]{:S(2)}) copy-start(bf16[192,1536]{1,0:T(8,128)(2,1)} %vit_out_hbm.1) | copy-start | bytes 1769476
  7.4 34.3 %copy-start.5 = (bf16[128,768]{1,0:T(8,128)(2,1)S(1)}, bf16[128,768]{1,0:T(8,128)(2,1)}, u32[]{:S(2)}) copy-start(bf16[128,768]{1,0:T(8,128)(2,1)} %cached_hbm.1) | copy-start | bytes 589828
  7.4 34.3 %copy-start.6 = (s32[256]{0:T(256)S(1)}, s32[256]{0:T(256)}, u32[]{:S(2)}) copy-start(s32[256]{0:T(256)} %param.17) | copy-start | bytes 3076
  7.5 34.3 %copy-start.7 = (s32[4]{0:T(128)S(1)}, s32[4]{0:T(128)}, u32[]{:S(2)}) copy-start(s32[4]{0:T(128)} %slide_tiles_ref.1) | copy-start | bytes 52
  7.5 34.3 %copy-start.8 = (s32[16]{0:T(128)S(1)}, s32[16]{0:T(128)}, u32[]{:S(2)}) copy-start(s32[16]{0:T(128)} %head_shift_ref.1) | copy-start | bytes 196
where the time goes:
time: 96.9 us; the launch traced here: 96.7 us
  Pallas kernels  88.5 us (91%)
  local copies, waits for them, and re-layouts  8.14 us (8%)
    pallas_call x1, Pallas kernels, slide_layer(): pl.pallas_call(slide_kernel, out_shape=jax.ShapeDtypeStruct((ROWS, LD), B...  54.2 us
    pallas_call x1, Pallas kernels, encode_tiles(): pl.pallas_call(tile_kernel, grid=(TILES_HERE,), in_specs=[pl.BlockSpec((1...  34.3 us
    unnamed x19, local copies, waits for them, and re-layouts  6.76 us

commit v1 on v0

--- a/solution.py
+++ b/solution.py
@@ -32,6 +32,9 @@
 SEG = 1024
 CHUNK = 2048
 KX = 64
+GROUP = 2
+WIDE = GROUP * TOK
+AHEAD = 4
 VIT_SCALE = LOG2E / math.sqrt(VS)
 LONG_SCALE = LOG2E / math.sqrt(LS)
 
@@ -52,90 +55,23 @@
     return high, middle, low
 
 
-def tile_kernel(x_ref, w_ref, pooled_ref, mean_ref, wext, csum):
-    step = pl.program_id(0)
-    tensor = lax.axis_index("tensor")
-
-    @pl.when(step == 0)
-    def _():
-        wext[0:VW, :] = w_ref[...]
-        row = iota((16, D), 0)
-        col = iota((16, D), 1)
-        extra = jnp.where(row == 0, 1.0, jnp.where((row == 1) & (col == 0), 1.0, 0.0))
-        wext[VW : VW + 16, :] = extra.astype(BF16)
-        csum[...] = dot(w_ref[...], jnp.ones((D, TOK), BF16))
-
-    x = x_ref[0]
-    raw = dot(wext[...], x, NT)
-    mean = raw[VW : VW + 1] * (1.0 / D)
-    first_row = raw[VW + 1 : VW + 2]
-    first = x[:, 0:1].astype(F32)
-    squares = jnp.zeros((TOK, 128), F32)
-    for k in range(D // 128):
-        delta = x[:, 128 * k : 128 * (k + 1)].astype(F32) - first
-        squares = squares + delta * delta
-    high, middle, low = split3(squares)
-    ones = jnp.ones((16, 128), BF16)
-    total = dot(ones, high, NT) + dot(ones, middle, NT) + dot(ones, low, NT)
-    shift = mean - first_row
-    variance = jnp.maximum(total[0:1] * (1.0 / D) - shift * shift, 0.0)
-    scale = lax.rsqrt(variance + EPSILON)
-    projected = ((raw[0:VW] - csum[...] * mean) * scale).astype(BF16)
-    attended = []
-    for head in range(VH_HERE):
-        base = head * 3 * VS
-        query = projected[base : base + VS]
-        key = projected[base + VS : base + 2 * VS]
-        value = projected[base + 2 * VS : base + 3 * VS]
-        scores = dot(key, query, TN)
-        highest = jnp.max(scores, axis=0, keepdims=True)
-        weights = jnp.exp2((scores - highest) * VIT_SCALE)
-        sums = jnp.sum(weights, axis=0, keepdims=True)
-        mixture = dot(value, weights.astype(BF16))
-        attended.append((mixture / sums).astype(BF16))
-    attended = jnp.concatenate(attended, axis=0)
-    pooled = dot(jnp.ones((16, TOK), BF16), attended, NT) * (1.0 / TOK)
-    pooled_ref[pl.ds(step, 1), :] = pooled[0:1]
-
-    @pl.when(step // 2 == tensor)
-    def _():
-        sums = dot(jnp.ones((16, TOK), BF16), x) * (1.0 / TOK)
-        mean_ref[pl.ds(step % 2, 1), :] = sums[0:1]
-
-
-def encode_tiles(tokens, weights):
-    return pl.pallas_call(
-        tile_kernel,
-        grid=(TILES_HERE,),
-        in_specs=[
-            pl.BlockSpec((1, TOK, D), lambda i: (i, 0, 0)),
-            pl.BlockSpec((VW, D), lambda i: (0, 0)),
-        ],
-        out_specs=[
-            pl.BlockSpec((TILES_HERE, VH_HERE * VS), lambda i: (0, 0)),
-            pl.BlockSpec((8, D), lambda i: (0, 0)),
-        ],
-        out_shape=[
-            jax.ShapeDtypeStruct((TILES_HERE, VH_HERE * VS), F32),
-            jax.ShapeDtypeStruct((8, D), F32),
-        ],
-        scratch_shapes=[pltpu.VMEM((VW + 16, D), BF16), pltpu.VMEM((VW, TOK), F32)],
-        compiler_params=pltpu.CompilerParams(vmem_limit_bytes=32 * 1024 * 1024),
-    )(tokens, weights)
-
-
 def normalize_rows(values):
     center = values - jnp.mean(values, axis=-1, keepdims=True)
     return center * lax.rsqrt(jnp.mean(center * center, axis=-1, keepdims=True) + EPSILON)
 
 
+def whole_row(ref):
+    rows = ref[...].astype(F32)
+    return jnp.concatenate([rows[k : k + 1] for k in range(rows.shape[0])], axis=1)
+
+
 def bit_reversed(rank):
     return (rank % 2) * 8 + (rank // 2 % 2) * 4 + (rank // 4 % 2) * 2 + rank // 8
 
 
-def slide_kernel(
-    pooled_ref,
-    tile_mean_ref,
+def whole_kernel(
+    tokens_hbm,
+    vit_qkv_hbm,
     vit_out_hbm,
     tile_gain_ref,
     fresh_proj_hbm,
@@ -147,6 +83,12 @@
     long_qkv_hbm,
     long_out_hbm,
     out_ref,
+    tokens,
+    vit_qkv,
+    csum,
+    projected,
+    attended,
+    token_mean,
     vit_out,
     fresh_proj,
     cached,
@@ -174,6 +116,7 @@
     top,
     mix_out,
     mix_in,
+    token_sem,
     load_sem,
     sems,
 ):
@@ -206,6 +149,14 @@
     for k in range(1, 16):
         pl.semaphore_signal(barrier, 1, device_id=((d + k) % 16, t), device_id_type=MESH)
 
+    vit_load = pltpu.make_async_copy(vit_qkv_hbm, vit_qkv.at[0:VW], load_sem.at[5])
+    vit_load.start()
+    token_loads = [
+        pltpu.make_async_copy(tokens_hbm.at[i], tokens.at[i], token_sem.at[i])
+        for i in range(TILES_HERE)
+    ]
+    for load in token_loads[:AHEAD]:
+        load.start()
     loads = [
         pltpu.make_async_copy(src, dst, load_sem.at[i])
         for i, (src, dst) in enumerate(
@@ -218,24 +169,11 @@
             ]
         )
     ]
-    for load in loads:
-        load.start()
-
-    loads[0].wait()
-    high, middle, low = split3(pooled_ref[...])
-    weight = vit_out[...]
-    partial = dot(high, weight) + dot(middle, weight) + dot(low, weight)
-    for k in range(8):
-        part[k] = partial[2 * k : 2 * k + 2]
-    pl.semaphore_wait(barrier, 29)
-    reduce_copies = []
-    for k in range(1, 8):
-        peer = (t + k) % 8
-        copy = remote(part.at[peer], part_in.at[t], (d, peer))
-        copy.start()
-        reduce_copies.append(copy)
-    part_in[pl.ds(t, 1)] = part[pl.ds(t, 1)]
-
+
+    row = iota((16, D), 0)
+    col = iota((16, D), 1)
+    extra = jnp.where(row == 0, 1.0, jnp.where((row == 1) & (col == 0), 1.0, 0.0))
+    vit_qkv[VW : VW + 16, :] = extra.astype(BF16)
     shift = head_shift_ref[mine] % 16
     place = iota((SEG, 1), 0)
     goal = bit_reversed((place + 16 - shift) % 16) * 64 + place // 16
@@ -270,12 +208,98 @@
     def value_marks(count):
         return jnp.where(iota((16, count), 0) == 0, 1.0, 0.0).astype(BF16)
 
+    qx[LS:KX, :] = query_marks(CHUNK, SEG, chunk)
+    kx[LS:KX, :] = key_marks(CHUNK, SEG, chunk)
+    vx[LS:KX, :] = value_marks(CHUNK)
+
+
+    vit_load.wait()
+    csum[...] = dot(vit_qkv[0:VW], jnp.ones((D, 128), BF16))
+
+    def project(group):
+        for i in range(GROUP):
+            token_loads[group * GROUP + i].wait()
+        for i in range(GROUP):
+            after = group * GROUP + i + AHEAD
+            if after < TILES_HERE:
+                token_loads[after].start()
+        x = tokens[group * GROUP : (group + 1) * GROUP].reshape(WIDE, D)
+        raw = dot(vit_qkv[...], x, NT)
+        mean = raw[VW : VW + 1] * (1.0 / D)
+        shift_row = mean - raw[VW + 1 : VW + 2]
+        first = x[:, 0:1].astype(F32)
+        squares = jnp.zeros((WIDE, 128), F32)
+        for k in range(D // 128):
+            delta = x[:, 128 * k : 128 * (k + 1)].astype(F32) - first
+            squares = squares + delta * delta
+        ones = jnp.ones((16, 128), BF16)
+        total = sum(dot(ones, piece, NT) for piece in split3(squares))
+        variance = jnp.maximum(total[0:1] * (1.0 / D) - shift_row * shift_row, 0.0)
+        scale = lax.rsqrt(variance + EPSILON)
+        spread = jnp.concatenate([csum[...]] * (WIDE // 128), axis=1)
+        projected[group % 2] = ((raw[0:VW] - spread * mean) * scale).astype(BF16)
+
+    def attention(group):
+        for i in range(GROUP):
+            lanes = slice(i * TOK, (i + 1) * TOK)
+
+            def piece(head, which):
+                first = (head * 3 + which) * VS
+                return projected[group % 2, first : first + VS, lanes]
+
+            heads = range(VH_HERE)
+            scores = [dot(piece(head, 1), piece(head, 0), TN) for head in heads]
+            highest = [jnp.max(score, axis=0, keepdims=True) for score in scores]
+            weights = [
+                jnp.exp2((score - high) * VIT_SCALE) for score, high in zip(scores, highest)
+            ]
+            sums = [jnp.sum(weight, axis=0, keepdims=True) for weight in weights]
+            mixed = [
+                dot(piece(head, 2), weights[head].astype(BF16)) for head in heads
+            ]
+            place = (group * GROUP + i) * TOK
+            for head in heads:
+                attended[head * VS : (head + 1) * VS, place : place + TOK] = (
+                    mixed[head] / sums[head]
+                ).astype(BF16)
+
+    groups = TILES_HERE // GROUP
+    project(0)
+    for group in range(groups):
+        if group + 1 < groups:
+            project(group + 1)
+        else:
+            for load in loads:
+                load.start()
+        attention(group)
+    for i in range(2):
+        sums = dot(jnp.ones((16, TOK), BF16), tokens[2 * t + i])
+        token_mean[i : i + 1, :] = sums[0:1] * (1.0 / TOK)
+    tile_of = iota((TILES_HERE, TILES_HERE * TOK), 1) // TOK
+    picks = jnp.where(iota(tile_of.shape, 0) == tile_of, 1.0 / TOK, 0.0).astype(BF16)
+    pooled_term = dot(picks, attended[...], NT)
+
+    loads[0].wait()
+    high, middle, low = split3(pooled_term)
+    weight = vit_out[...]
+    partial = dot(high, weight) + dot(middle, weight) + dot(low, weight)
+    for k in range(8):
+        part[k] = partial[2 * k : 2 * k + 2]
+    pl.semaphore_wait(barrier, 29)
+    reduce_copies = []
+    for k in range(1, 8):
+        peer = (t + k) % 8
+        copy = remote(part.at[peer], part_in.at[t], (d, peer))
+        copy.start()
+        reduce_copies.append(copy)
+    part_in[pl.ds(t, 1)] = part[pl.ds(t, 1)]
+
     for copy in reduce_copies:
         copy.wait_recv()
-    pooled = tile_mean_ref[0:2, :]
+    pooled = token_mean[0:2, :]
     for k in range(8):
         pooled = pooled + part_in[k]
-    normed = (normalize_rows(pooled) * tile_gain_ref[...].astype(F32)).astype(BF16)
+    normed = (normalize_rows(pooled) * whole_row(tile_gain_ref)).astype(BF16)
     loads[1].wait()
     fresh = dot(normed, fresh_proj[...])
     fresh_in[pl.ds(t, 1)] = fresh[None]
@@ -302,7 +326,7 @@
         copy.wait_recv()
     rows = cached[...].astype(F32) + dot(match, fresh_all[...])
     seq[...] = rows
-    hidden[...] = (normalize_rows(rows) * long_gain_ref[...].astype(F32)).astype(BF16)
+    hidden[...] = (normalize_rows(rows) * whole_row(long_gain_ref)).astype(BF16)
 
     loads[3].wait()
     head_copies = []
@@ -350,10 +374,6 @@
         far_copies.append(remote(send4, got4.at[k], (2 * other + half, t)))
     for copy in far_copies:
         copy.start()
-
-    qx[LS:KX, :] = query_marks(CHUNK, SEG, chunk)
-    kx[LS:KX, :] = key_marks(CHUNK, SEG, chunk)
-    vx[LS:KX, :] = value_marks(CHUNK)
 
     def attend(keys, values, queries):
         scores = dot(keys, queries, TN)
@@ -484,16 +504,22 @@
             copy.wait_send()
 
 
-def slide_layer(*arguments):
+def whole_layer(*arguments):
     vmem = pl.BlockSpec(memory_space=pltpu.VMEM)
     smem = pl.BlockSpec(memory_space=pltpu.SMEM)
     hbm = pl.BlockSpec(memory_space=pl.ANY)
     return pl.pallas_call(
-        slide_kernel,
+        whole_kernel,
         out_shape=jax.ShapeDtypeStruct((ROWS, LD), BF16),
-        in_specs=[vmem, vmem, hbm, vmem, hbm, vmem, hbm, smem, smem, vmem, hbm, hbm],
+        in_specs=[hbm, hbm, hbm, vmem, hbm, vmem, hbm, smem, smem, vmem, hbm, hbm],
         out_specs=vmem,
         scratch_shapes=[
+            pltpu.VMEM((TILES_HERE, TOK, D), BF16),
+            pltpu.VMEM((VW + 16, D), BF16),
+            pltpu.VMEM((VW, 128), F32),
+            pltpu.VMEM((2, VW, WIDE), BF16),
+            pltpu.VMEM((VH_HERE * VS, TILES_HERE * TOK), BF16),
+            pltpu.VMEM((8, D), F32),
             pltpu.VMEM((VH_HERE * VS, D), BF16),
             pltpu.VMEM((D, LD), BF16),
             pltpu.VMEM((ROWS, LD), BF16),
@@ -521,13 +547,14 @@
             pltpu.VMEM((8, CHUNK), F32),
             pltpu.VMEM((16, LS, ROWS), BF16),
             pltpu.VMEM((16, LS, ROWS), BF16),
-            pltpu.SemaphoreType.DMA((5,)),
+            pltpu.SemaphoreType.DMA((TILES_HERE,)),
+            pltpu.SemaphoreType.DMA((6,)),
             pltpu.SemaphoreType.DMA((2, 66)),
         ],
         compiler_params=pltpu.CompilerParams(
             collective_id=0,
             has_side_effects=True,
-            vmem_limit_bytes=48 * 1024 * 1024,
+            vmem_limit_bytes=60 * 1024 * 1024,
         ),
     )(*arguments)
 
@@ -548,18 +575,17 @@
 ):
     vit_rows = jnp.transpose(vit_qkv, (1, 2, 3, 0)).reshape(VW, D)
     long_rows = jnp.transpose(long_qkv, (1, 2, 3, 0)).reshape(LH * LW, LD)
-    pooled, tile_means = encode_tiles(tile_tokens, vit_rows)
-    return slide_layer(
-        pooled,
-        tile_means,
+    return whole_layer(
+        tile_tokens,
+        vit_rows,
         vit_out,
-        tile_norm_gain.reshape(1, D),
+        tile_norm_gain.reshape(D // 128, 128),
         fresh_proj,
         tile_target.reshape(1, 256),
         cached_rows,
         slide_tiles,
         head_shift,
-        long_gain.reshape(1, LD),
+        long_gain.reshape(LD // 128, 128),
         long_rows,
         long_out,
     )

time: 96.9 us -> 76.7 us (0.79)
  Pallas kernels: 88.5 us -> 74.9 us
  local copies, waits for them, and re-layouts: 8.14 us -> 1.62 us
    pallas_call x2 -> x1, Pallas kernels: 88.5 us -> 74.9 us  [whole_layer(): pl.pallas_call(whole_kernel, out_shape=jax.ShapeDtypeStruct((ROWS, LD), B...]
    unnamed x19 -> x1, local copies, waits for them, and re-layouts: 6.76 us -> 1.62 us
    reshape x2 -> x0, local copies, waits for them, and re-layouts: 1.38 us -> none  [the longest x1 0.69 us: body(): tile_norm_gain.reshape(1, D)]
where the time goes in v1:
time: 76.7 us; the launch traced here: 76.5 us
  Pallas kernels  74.9 us (98%)
  local copies, waits for them, and re-layouts  1.62 us (2%)
    pallas_call x1, Pallas kernels, whole_layer(): pl.pallas_call(whole_kernel, out_shape=jax.ShapeDtypeStruct((ROWS, LD), B...  74.9 us
    unnamed x1, local copies, waits for them, and re-layouts  1.62 us

profile of v1, /device:TPU:1, one launch (start us, length us, event | category | flops | bytes accessed | tf_op | source)
XLA Modules:
  0.0 76.5 jit_solution(10171274083119490559)
XLA Ops:
  0.0 74.9 %shard_map.118 = bf16[128,768]{1,0:T(8,128)(2,1)} custom-call(bf16[16,256,1536]{2,1,0:T(8,128)(2,1)} %tokens_hbm.1, bf16[576,1536]{1,0:T(8,128)(2,1)} %bitcast.10, bf16[192,1536]{1,0:T(8,128)(2,1)} %vit_out_hbm.1, bf16[12,128]{1,0:T(8,128)(2,1)} %bitcast.11, bf16[1536,768]{1,0:T(8,128)(2,1)} %fresh_proj_hbm.1, s32[1,256]{1,0:T(1,128)} %bitcast.13, ...), custom_call_target="tpu_custom_call" | custom-call | tf_op jit(solution)/shard_map/pallas_call | solution.py:511
  74.9 1.6 %copy.14 = bf16[128,768]{1,0:T(8,128)(2,1)} copy(bf16[128,768]{1,0:T(8,128)(2,1)} %shard_map.118) | data formatting | bytes 393216
